TPU v7x, 32 devices: a whole 2x2x4 slice. The times are simulated.
32 devices in a mesh: groups: 2 (over x), member: 16 (over z, y, core).
Axes of the slice: x: 2, y: 2, z: 4, core: 2. Of those that a mesh axis runs over, the one named last changes fastest.
Arguments:
- tile_values: bfloat16 [32, 64, 4, 128, 128], P(('groups', 'member')), parts along dimension 0, may hold values from -0.25 to 0.25
- directions: bfloat16 [32, 24, 8192], P(('groups', 'member')), parts along dimension 0, may hold values from -6 to 6
- columns: int32 [64, 4], replicated, may hold values from 0 to 63
- counts: int32 [64], replicated, may hold values from 1 to 4, as said below
- weights: float32 [8192], replicated, may hold values from 2.4414063e-05 to 0.00024414062
Outputs:
- gram_rows: float32 [768, 384], P(('groups', 'member')), parts along dimension 0
There are 2 independent parts, one for each index of `groups`. A program takes and returns all parts, laid end to end along the dimension named above; an argument that names none is the same for every part. Nothing has to cross between parts.
Inputs may be any that keep to these rules, and one draw needn't show every extreme that they name: `counts`: some row tile has all 4 slots live.
All inputs are finite; a program needn't handle non-finite values.
Results may differ from a plain program's by a relative error of at most 0.0013.
Values may be sent and summed in bfloat16 or wider, within the bound.
A program may use at most 64 MiB of HBM per device.

v0:
```python
import jax
import jax.numpy as jnp
from jax import lax
from jax.sharding import PartitionSpec as P


def snapshot(tiles_one, dirs_one, columns, counts):
    row_tiles, per_row, tile_size, _ = tiles_one.shape
    snaps = dirs_one.shape[0]
    blocks = dirs_one.reshape(snaps, row_tiles, tile_size)
    picked = blocks[:, columns, :]
    slot_ids = lax.broadcasted_iota(jnp.int32, (row_tiles, per_row), 1)
    live_mask = (slot_ids < counts[:, None]).astype(jnp.bfloat16)
    picked = picked * live_mask[None, :, :, None]
    result = jnp.einsum("rkij,srkj->sri", tiles_one, picked, preferred_element_type=jnp.float32)
    return result.reshape(snaps, row_tiles * tile_size).astype(jnp.bfloat16)


def per_device(tile_values, directions, columns, counts, weights):
    snaps_local = snapshot(tile_values[0], directions[0], columns, counts)
    regrouped = lax.all_to_all(snaps_local, "member", split_axis=1, concat_axis=0, tiled=True)
    width = regrouped.shape[1]
    offset = lax.axis_index("member") * width
    row_weights = lax.dynamic_slice_in_dim(weights, offset, width, 0)
    weighted = (regrouped.astype(jnp.float32) * row_weights[None, :]).astype(jnp.bfloat16)
    return lax.psum_scatter(
        lax.dot_general(
            weighted, regrouped, (((1,), (1,)), ((), ())), preferred_element_type=jnp.float32
        ),
        "member",
        scatter_dimension=0,
        tiled=True,
    )


def solution(mesh):
    in_specs = (
        P(("groups", "member"), None, None, None, None),
        P(("groups", "member"), None, None),
        P(),
        P(),
        P(),
    )
    out_specs = P(("groups", "member"), None)
    return jax.shard_map(
        per_device, mesh=mesh, in_specs=in_specs, out_specs=out_specs, check_vma=False
    )
```

profile of v0, /device:TPU:0, one launch (start us, length us, event | category | flops | bytes accessed | tf_op | source)
XLA Modules:
  0.0 97.9 jit_solution(11330450810175863388)
XLA Ops:
  6.5 0.0 copy-start
  6.5 0.0 copy-start.1
  6.5 1.1 %copy.21 = bf16[3,8,64,128]{3,2,1,0:T(8,128)(2,1)S(1)} copy(bf16[3,8,64,128]{3,1,2,0:T(8,128)(2,1)} %bitcast.43) | data formatting | bytes 786432
  7.6 0.3 copy.17
  7.9 0.0 copy-done
  7.9 0.1 copy.16
  8.0 0.1 reshape.34
  8.2 0.0 copy-done.1
  8.2 0.1 fusion.20
  8.2 1.0 %gather_fusion = bf16[256,24,128]{2,1,0:T(8,128)(2,1)S(1)} fusion(bf16[24,64,128]{2,0,1:T(8,128)(2,1)S(1)} %copy.17, s32[1024]{0:T(1024)S(1)} %pad_clamp_fusion), kind=kCustom, calls=%fused_computation | custom fusion | bytes 3146752 | tf_op jit(solution)/shard_map/gather | solution.py:11
  9.2 5.7 %fusion.14 = bf16[24,64,128]{2,0,1:T(8,128)(2,1)S(1)} fusion(bf16[1,64,4,128,128]{4,3,2,1,0:T(8,128)(2,1)} %param.5, bf16[64,4,24,128]{3,2,1,0:T(8,128)(2,1)S(1)} %bitcast.39, bf16[64,4]{1,0:T(8,128)(2,1)S(1)} %fusion.20), kind=kOutput, calls=%fused_computation.7 | convolution fusion | flops 202309632 | bytes 10355200 | tf_op jit(solution)/shard_map/rkij,srkj->sri/dot_general | solution.py:15
  14.9 0.1 copy.18
  15.0 0.2 convert_element_type.30
  15.3 1.0 copy.19
  16.3 7.4 %all-to-all-start = ((bf16[24,16,512]{2,0,1:T(8,128)(2,1)}), bf16[24,16,512]{2,0,1:T(8,128)(2,1)S(1)}, u32[]{:S(2)}, u32[]{:S(2)}) async-start(bf16[24,16,512]{2,0,1:T(8,128)(2,1)} %copy.19), calls=%async_computation | async-start | bytes 786432 | tf_op jit(solution)/shard_map/all_to_all | solution.py:21
  23.6 0.0 reduce-scatter.4.cloned.1.call-start
  23.7 0.8 dynamic_slice.3
  24.5 11.4 %all-to-all-done = bf16[24,16,512]{2,0,1:T(8,128)(2,1)S(1)} async-done(((bf16[24,16,512]{2,0,1:T(8,128)(2,1)}), bf16[24,16,512]{2,0,1:T(8,128)(2,1)S(1)}, u32[]{:S(2)}, u32[]{:S(2)}) %all-to-all-start) | async-done | bytes 393248 | tf_op jit(solution)/shard_map/all_to_all | solution.py:21
  35.8 0.1 multiply_convert_fusion
  35.9 1.2 %fusion.21 = f32[384,384]{1,0:T(8,128)} fusion(bf16[384,512]{1,0:T(8,128)(2,1)S(1)} %bitcast.42, bf16[384,512]{1,0:T(8,128)(2,1)S(1)} %bitcast.40), kind=kOutput, calls=%fused_computation.14 | convolution fusion | flops 150994944 | bytes 1376256 | tf_op jit(solution)/shard_map/dot_general | solution.py:27
  37.1 0.0 reduce-scatter.4.cloned.1.call-update
  37.2 53.9 %reduce-scatter.4.cloned.1.call-done = f32[24,384]{1,0:T(8,128)} async-done(((f32[384,384]{1,0:T(8,128)}), f32[24,384]{1,0:T(8,128)}) %reduce-scatter.4.cloned.1.call-update) | async-done | bytes 36880
  (2 shorter events, 0.0 us)
Async XLA Ops:
  6.5 1.4 %copy-start = (s32[64,4]{0,1:T(4,128)S(1)}, s32[64,4]{0,1:T(4,128)}, u32[]{:S(2)}) copy-start(s32[64,4]{0,1:T(4,128)} %param.7) | copy-start | bytes 3076
  6.5 1.6 %copy-start.1 = (s32[64]{0:T(128)S(1)}, s32[64]{0:T(128)}, u32[]{:S(2)}) copy-start(s32[64]{0:T(128)} %param.8) | copy-start | bytes 772
  16.3 19.6 %all-to-all-start = ((bf16[24,16,512]{2,0,1:T(8,128)(2,1)}), bf16[24,16,512]{2,0,1:T(8,128)(2,1)S(1)}, u32[]{:S(2)}, u32[]{:S(2)}) async-start(bf16[24,16,512]{2,0,1:T(8,128)(2,1)} %copy.19), calls=%async_computation | async-start | bytes 786432 | tf_op jit(solution)/shard_map/all_to_all | solution.py:21
  23.6 67.4 %reduce-scatter.4.cloned.1.call-start = ((), (), s32[]{:S(2)}) async-start(), calls=%async_computation.2 | async-start | bytes 626688
Sparse Core Ops, SparseCore 0:
  37.3 53.7 reduce-scatter.3
where the time goes:
time: 98.1 us; the launch traced here: 97.9 us
  waiting for transfers between devices  65.3 us (67%)
  between operations  13.5 us (14%)
  starting transfers between devices  7.43 us (8%)
  matrix products  6.93 us (7%)
  local copies, waits for them, and re-layouts  4.62 us (5%)
    unnamed x2, waiting for transfers between devices  53.9 us
    all_to_all x1, waiting for transfers between devices, per_device(): lax.all_to_all(snaps_local, 'member', split_axis=1, concat_axis=0, tiled=...  11.4 us
    all_to_all x1, starting transfers between devices, per_device(): lax.all_to_all(snaps_local, 'member', split_axis=1, concat_axis=0, tiled=...  7.39 us
    dot_general x1, matrix products, snapshot(): jnp.einsum('rkij,srkj->sri', tiles_one, picked, preferred_element_type=jn...  5.71 us
  transfers between devices with their start and end apart: 2, of which 2 were waited for; matrix products, arithmetic and copies ran while one was open for 1% of the time, Pallas kernels for 0%

commit v1 on v0

v1 whole, which is shorter than its diff:
```python
import functools

import jax
import jax.numpy as jnp
from jax import lax
from jax.experimental import pallas as pl
from jax.experimental.pallas import tpu as pltpu
from jax.sharding import PartitionSpec as P

MESH = pl.DeviceIdType.MESH
LANES = 128


def kernel(n, fold, tiles_hbm, dirs_ref, cols_ref, counts_ref, weights_ref, out_ref,
           tiles, dirs, snap_out, snap_in, gram, gram_out, gram_in,
           tile_sem, send1, recv1, send2, recv2):
    me = lax.axis_index("member")
    row_tiles, per_row = cols_ref.shape
    snaps = dirs_ref.shape[1]
    chunk = row_tiles // n
    half = n // 2
    strips = n * snaps // LANES

    def nth(step):
        off = half + (step % 2) * ((step + 1) // 2) - ((step + 1) % 2) * (step // 2)
        return lax.rem(me + off, n)

    def tile_copy(step):
        rows = pl.ds(nth(step) * chunk, chunk)
        return pltpu.make_async_copy(tiles_hbm.at[0, rows], tiles.at[rows], tile_sem.at[step])

    def snap_copy(dest, source):
        return pltpu.make_async_remote_copy(
            src_ref=snap_out.at[dest], dst_ref=snap_in.at[source],
            send_sem=send1.at[dest], recv_sem=recv1.at[source],
            device_id={"member": dest}, device_id_type=MESH)

    def gram_copy(dest, source):
        return pltpu.make_async_remote_copy(
            src_ref=gram_out.at[dest], dst_ref=gram_in.at[source],
            send_sem=send2.at[dest], recv_sem=recv2.at[source],
            device_id={"member": dest}, device_id_type=MESH)

    def start_tiles(step, carry):
        tile_copy(step).start()
        return carry

    lax.fori_loop(0, n, start_tiles, 0)

    barrier = pltpu.get_barrier_semaphore()

    def greet(off, carry):
        pl.semaphore_signal(barrier, inc=1, device_id={"member": lax.rem(me + off, n)},
                            device_id_type=MESH)
        return carry

    lax.fori_loop(1, n, greet, 0)

    for c in range(row_tiles):
        dirs[c] = dirs_ref[0, :, c * LANES:(c + 1) * LANES]
    dirs[row_tiles] = jnp.zeros(dirs.shape[1:], dirs.dtype)

    def product(dest):
        parts = []
        for t in range(chunk):
            r = dest * chunk + t
            picked = []
            for k in range(per_row):
                picked.append(dirs[jnp.where(k < counts_ref[r], cols_ref[r, k], row_tiles)])
            lhs = jnp.concatenate(picked, axis=1)
            rhs = jnp.concatenate([tiles[r, k] for k in range(per_row)], axis=1)
            parts.append(lax.dot_general(lhs, rhs, (((1,), (1,)), ((), ())),
                                         preferred_element_type=jnp.float32))
        each = chunk // fold
        rows = [jnp.concatenate(parts[f * each:(f + 1) * each], axis=1) for f in range(fold)]
        return jnp.concatenate(rows, axis=0).astype(jnp.bfloat16)

    def one(step):
        tile_copy(step).wait()
        dest = nth(step)
        snap_out[dest] = product(dest)
        snap_copy(dest, me).start()

    tile_copy(0).wait()
    first = nth(0)
    snap_out[first] = product(first)
    pl.semaphore_wait(barrier, n - 1)
    snap_copy(first, me).start()

    def body(step, carry):
        one(step)
        return carry

    lax.fori_loop(1, n - 1, body, 0)
    tile_copy(n - 1).wait()
    snap_in[me] = product(me)

    def land(step, carry):
        snap_copy(me, nth(step)).wait_recv()
        return carry

    lax.fori_loop(0, n - 1, land, 0)

    each = chunk // fold
    flats, weighteds = [], []
    for f in range(fold):
        for t in range(each):
            got = snap_in[:, :, t * LANES:(t + 1) * LANES].astype(jnp.float32)
            flat = got[:, f * snaps:(f + 1) * snaps].reshape(n * snaps, LANES)
            w = weights_ref[pl.ds(me * chunk + f * each + t, 1), :]
            flats.append(flat.astype(jnp.bfloat16))
            weighteds.append((flat * w).astype(jnp.bfloat16))
    total = lax.dot_general(jnp.concatenate(weighteds, axis=1), jnp.concatenate(flats, axis=1),
                            (((1,), (1,)), ((), ())), preferred_element_type=jnp.float32)
    gram[...] = total.reshape(n, snaps, n * snaps)

    def give(step, carry):
        dest = nth(step)
        block = gram[dest]
        gram_out[dest] = jnp.concatenate(
            [block[:, c * LANES:(c + 1) * LANES] for c in range(strips)], axis=0
        ).astype(jnp.bfloat16)
        gram_copy(dest, me).start()
        return carry

    lax.fori_loop(0, n - 1, give, 0)
    out_ref[...] = gram[me]

    def take(step, carry):
        source = nth(step)
        gram_copy(me, source).wait_recv()
        got = gram_in[source].astype(jnp.float32)
        out_ref[...] += jnp.concatenate(
            [got[c * snaps:(c + 1) * snaps] for c in range(strips)], axis=1)
        return carry

    lax.fori_loop(0, n - 1, take, 0)

    def drain(step, carry):
        snap_copy(nth(step), me).wait_send()
        gram_copy(nth(step), me).wait_send()
        return carry

    lax.fori_loop(0, n - 1, drain, 0)


def per_device(n, tile_values, directions, columns, counts, weights):
    _, row_tiles, per_row, size, _ = tile_values.shape
    snaps = directions.shape[1]
    chunk = row_tiles // n
    fold = 2 if chunk % 2 == 0 else 1
    strips = n * snaps // LANES
    message = (n, fold * snaps, chunk * size // fold)
    block = (n, strips * snaps, LANES)
    vmem = pl.BlockSpec(memory_space=pltpu.VMEM)
    smem = pl.BlockSpec(memory_space=pltpu.SMEM)
    return pl.pallas_call(
        functools.partial(kernel, n, fold),
        out_shape=jax.ShapeDtypeStruct((snaps, n * snaps), jnp.float32),
        in_specs=[pl.BlockSpec(memory_space=pl.ANY), vmem, smem, smem, vmem],
        out_specs=vmem,
        scratch_shapes=[
            pltpu.VMEM((row_tiles, per_row, size, size), jnp.bfloat16),
            pltpu.VMEM((row_tiles + 1, snaps, size), jnp.bfloat16),
            pltpu.VMEM(message, jnp.bfloat16),
            pltpu.VMEM(message, jnp.bfloat16),
            pltpu.VMEM((n, snaps, n * snaps), jnp.float32),
            pltpu.VMEM(block, jnp.bfloat16),
            pltpu.VMEM(block, jnp.bfloat16),
            pltpu.SemaphoreType.DMA((n,)),
            pltpu.SemaphoreType.DMA((n,)),
            pltpu.SemaphoreType.DMA((n,)),
            pltpu.SemaphoreType.DMA((n,)),
            pltpu.SemaphoreType.DMA((n,)),
        ],
        compiler_params=pltpu.CompilerParams(
            collective_id=0, has_side_effects=True, vmem_limit_bytes=48 * 2**20),
    )(tile_values, directions, columns, counts, weights.reshape(-1, LANES))


def solution(mesh):
    in_specs = (
        P(("groups", "member"), None, None, None, None),
        P(("groups", "member"), None, None),
        P(),
        P(),
        P(),
    )
    out_specs = P(("groups", "member"), None)
    return jax.shard_map(
        functools.partial(per_device, mesh.shape["member"]), mesh=mesh,
        in_specs=in_specs, out_specs=out_specs, check_vma=False
    )
```

time: 98.1 us -> 31 us (0.32)
  waiting for transfers between devices: 65.3 us -> 0 us
  Pallas kernels: 0 us -> 27 us
  between operations: 13.5 us -> 0.01 us
  starting transfers between devices: 7.43 us -> 0 us
  matrix products: 6.93 us -> 0 us
    unnamed x2 -> x0, waiting for transfers between devices: 53.9 us -> none
    pallas_call x0 -> x1, Pallas kernels: none -> 27 us  [per_device(): pl.pallas_call(functools.partial(kernel, n, fold), out_shape=jax.ShapeDty...]
    all_to_all x1 -> x0, waiting for transfers between devices: 11.4 us -> none  [per_device(): lax.all_to_all(snaps_local, 'member', split_axis=1, concat_axis=0, tiled=...]
    all_to_all x1 -> x0, starting transfers between devices: 7.39 us -> none  [per_device(): lax.all_to_all(snaps_local, 'member', split_axis=1, concat_axis=0, tiled=...]
    dot_general x2 -> x0, matrix products: 6.93 us -> none  [the longest x1 5.71 us: snapshot(): jnp.einsum('rkij,srkj->sri', tiles_one, picked, preferred_element_type=jn...]
    unnamed x5 -> x8, local copies, waits for them, and re-layouts: 1.11 us -> 3.8 us
    convert_element_type x3 -> x0, local copies, waits for them, and re-layouts: 1.3 us -> none  [snapshot(): return result.reshape(snaps, row_tiles * tile_size).astype(jnp.bfloat16)]
    gather x1 -> x0, local copies, waits for them, and re-layouts: 0.99 us -> none  [snapshot(): picked = blocks[:, columns, :]]
  transfers between devices with their start and end apart: 2 -> 0, of which waited for: 2 -> 0; matrix products, arithmetic and copies ran while one was open for 1% -> 0% of each run, Pallas kernels for 0% -> 0%
where the time goes in v1:
time: 31 us; the launch traced here: 30.8 us
  Pallas kernels  27 us (87%)
  local copies, waits for them, and re-layouts  3.8 us (12%)
    pallas_call x1, Pallas kernels, per_device(): pl.pallas_call(functools.partial(kernel, n, fold), out_shape=jax.ShapeDty...  27 us
    unnamed x8, local copies, waits for them, and re-layouts  3.8 us

profile of v1, /device:TPU:0, one launch (start us, length us, event | category | flops | bytes accessed | tf_op | source)
XLA Modules:
  0.0 30.8 jit_solution(1453702380327485539)
XLA Ops:
  0.0 0.8 %copy.6.cols_ref = s32[64,4]{1,0:T(8,128)S(1)} copy(s32[64,4]{0,1:T(4,128)} %param.7) | data formatting | bytes 2048 | tf_op args[2]
  0.8 0.0 copy-start
  0.8 1.0 %copy-done = bf16[1,24,8192]{2,1,0:T(8,128)(2,1)S(1)} copy-done((bf16[1,24,8192]{2,1,0:T(8,128)(2,1)S(1)}, bf16[1,24,8192]{2,1,0:T(8,128)(2,1)}, u32[]{:S(2)}) %copy-start) | copy-done | bytes 393240
  1.8 0.0 copy-start.1
  1.8 0.8 %copy-done.1 = f32[8192]{0:T(1024)S(1)} copy-done((f32[8192]{0:T(1024)S(1)}, f32[8192]{0:T(1024)}, u32[]{:S(2)}) %copy-start.1) | copy-done | bytes 32792
  2.5 0.0 copy-start.2
  2.5 0.7 %copy-done.2 = s32[64]{0:T(128)S(1)} copy-done((s32[64]{0:T(128)S(1)}, s32[64]{0:T(128)}, u32[]{:S(2)}) %copy-start.2) | copy-done | bytes 280
  3.2 27.0 %shard_map.55 = f32[24,384]{1,0:T(8,128)S(1)} custom-call(bf16[1,64,4,128,128]{4,3,2,1,0:T(8,128)(2,1)} %tiles_hbm.1, bf16[1,24,8192]{2,1,0:T(8,128)(2,1)S(1)} %copy-done, s32[64,4]{1,0:T(8,128)S(1)} %copy.6.cols_ref, s32[64]{0:T(128)S(1)} %copy-done.2, f32[64,128]{1,0:T(8,128)S(1)} %bitcast.1), custom_call_target="tpu_custom_call" | custom-call | tf_op jit(solution)/shard_map/pallas_call | solution.py:157
  30.2 0.6 %copy.8 = f32[24,384]{1,0:T(8,128)} copy(f32[24,384]{1,0:T(8,128)S(1)} %shard_map.55) | data formatting | bytes 73728
Async XLA Ops:
  0.8 1.0 %copy-start = (bf16[1,24,8192]{2,1,0:T(8,128)(2,1)S(1)}, bf16[1,24,8192]{2,1,0:T(8,128)(2,1)}, u32[]{:S(2)}) copy-start(bf16[1,24,8192]{2,1,0:T(8,128)(2,1)} %dirs_ref.1) | copy-start | bytes 1179652
  1.8 0.8 %copy-start.1 = (f32[8192]{0:T(1024)S(1)}, f32[8192]{0:T(1024)}, u32[]{:S(2)}) copy-start(f32[8192]{0:T(1024)} %param.9) | copy-start | bytes 98308
  2.5 0.7 %copy-start.2 = (s32[64]{0:T(128)S(1)}, s32[64]{0:T(128)}, u32[]{:S(2)}) copy-start(s32[64]{0:T(128)} %counts_ref.1) | copy-start | bytes 772

commit v2 on v0

v2 whole, which is shorter than its diff:
```python
import functools

import jax
import jax.numpy as jnp
from jax import lax
from jax.experimental import pallas as pl
from jax.experimental.pallas import tpu as pltpu
from jax.sharding import PartitionSpec as P

MESH = pl.DeviceIdType.MESH
LANES = 128


def pack(block):
    snaps, columns = block.shape
    full = columns // LANES
    rows = [block[:, c * LANES:(c + 1) * LANES] for c in range(full)]
    if columns % LANES:
        rest = block[:, full * LANES:]
        left = rest[:16]
        right = jnp.concatenate([rest[16:], jnp.zeros((32 - snaps, LANES // 2), rest.dtype)], axis=0)
        rows.append(jnp.concatenate([left, right], axis=1))
    return jnp.concatenate(rows, axis=0)


def unpack(rows, snaps, columns):
    full = columns // LANES
    parts = [rows[c * snaps:(c + 1) * snaps] for c in range(full)]
    if columns % LANES:
        rest = rows[full * snaps:]
        parts.append(jnp.concatenate(
            [rest[:, :LANES // 2], rest[:snaps - 16, LANES // 2:]], axis=0))
    return jnp.concatenate(parts, axis=1)


def packed_rows(snaps, columns):
    return columns // LANES * snaps + (16 if columns % LANES else 0)


def kernel(n, fold, tiles_hbm, dirs_hbm, cols_hbm, counts_hbm, weights_hbm, out_ref,
           dirs_ref, cols_ref, counts_ref, weights_ref, tiles, dirs,
           snap_out, snap_own, snap_far, gram_own, gram_far, own_out, own_in, far_out, far_in,
           arg_sem, tile_sem, own_send1, own_recv1, far_send1, far_recv1,
           own_send2, own_recv2, far_send2, far_recv2):
    me = lax.axis_index("member")
    per_row, row_tiles = cols_ref.shape
    snaps = dirs_ref.shape[1]
    chunk = row_tiles // n
    each = chunk // fold
    half = n // 2
    side, loc = me // half, me % half
    mine, other = side * half, (1 - side) * half
    rows_half = half * snaps
    mid = half // 2

    def nth(step):
        off = mid + (step % 2) * ((step + 1) // 2) - ((step + 1) % 2) * (step // 2)
        return lax.rem(loc + off, half)

    def slab_start(spot, which):
        return (2 * spot + (side if which == 0 else 1 - side)) * chunk

    def tile_copy(step, which):
        rows = pl.ds(slab_start(nth(step), which), chunk)
        return pltpu.make_async_copy(
            tiles_hbm.at[0, rows], tiles.at[rows], tile_sem.at[which, step])

    def remote(src, dst, send, recv, dest):
        return pltpu.make_async_remote_copy(
            src_ref=src, dst_ref=dst, send_sem=send, recv_sem=recv,
            device_id={"member": dest}, device_id_type=MESH)

    def own_snap(spot, source):
        return remote(snap_out.at[spot], snap_own.at[source], own_send1.at[spot],
                      own_recv1.at[source], mine + spot)

    def far_snap(spot, source):
        return remote(snap_out.at[spot, 1], snap_far.at[source], far_send1.at[spot],
                      far_recv1.at[source], other + spot)

    def own_gram(spot, source):
        return remote(own_out.at[spot], own_in.at[source], own_send2.at[spot],
                      own_recv2.at[source], mine + spot)

    def far_gram(spot, source):
        return remote(far_out.at[spot], far_in.at[source], far_send2.at[spot],
                      far_recv2.at[source], other + spot)

    args = [
        pltpu.make_async_copy(a, b, arg_sem.at[i]) for i, (a, b) in enumerate(
            [(dirs_hbm, dirs_ref), (cols_hbm, cols_ref), (counts_hbm, counts_ref),
             (weights_hbm, weights_ref)])
    ]
    for copy in args:
        copy.start()

    def start_tiles(step, carry):
        tile_copy(step, 1).start()
        tile_copy(step, 0).start()
        return carry

    lax.fori_loop(0, half, start_tiles, 0)

    barrier = pltpu.get_barrier_semaphore()

    def greet(off, carry):
        pl.semaphore_signal(barrier, inc=1, device_id={"member": lax.rem(me + off, n)},
                            device_id_type=MESH)
        return carry

    lax.fori_loop(1, n, greet, 0)

    for copy in args:
        copy.wait()
    for c in range(row_tiles):
        dirs[c] = dirs_ref[0, :, c * LANES:(c + 1) * LANES]
    dirs[row_tiles] = jnp.zeros(dirs.shape[1:], dirs.dtype)

    def product(spot, which):
        parts = []
        for t in range(chunk):
            r = slab_start(spot, which) + t
            picked = [dirs[jnp.where(k < counts_ref[r], cols_ref[k, r], row_tiles)]
                      for k in range(per_row)]
            lhs = jnp.concatenate(picked, axis=1)
            rhs = jnp.concatenate([tiles[r, k] for k in range(per_row)], axis=1)
            parts.append(lax.dot_general(lhs, rhs, (((1,), (1,)), ((), ())),
                                         preferred_element_type=jnp.float32))
        rows = [jnp.concatenate(parts[f * each:(f + 1) * each], axis=1) for f in range(fold)]
        return jnp.concatenate(rows, axis=0).astype(jnp.bfloat16)

    first = nth(0)
    tile_copy(0, 1).wait()
    snap_out[first, 1] = product(first, 1)
    pl.semaphore_wait(barrier, n - 1)
    far_snap(first, loc).start()
    tile_copy(0, 0).wait()
    snap_out[first, 0] = product(first, 0)
    own_snap(first, loc).start()

    def body(step, carry):
        spot = nth(step)
        tile_copy(step, 1).wait()
        snap_out[spot, 1] = product(spot, 1)
        far_snap(spot, loc).start()
        tile_copy(step, 0).wait()
        snap_out[spot, 0] = product(spot, 0)
        own_snap(spot, loc).start()
        return carry

    lax.fori_loop(1, half - 1, body, 0)
    tile_copy(half - 1, 1).wait()
    last = product(loc, 1)
    snap_out[loc, 1] = last
    far_snap(loc, loc).start()
    snap_own[loc, 1] = last
    tile_copy(half - 1, 0).wait()
    snap_own[loc, 0] = product(loc, 0)

    def land(step, carry):
        own_snap(loc, nth(step)).wait_recv()
        far_snap(loc, nth(step)).wait_recv()
        return carry

    lax.fori_loop(0, half - 1, land, 0)
    far_snap(loc, loc).wait_recv()

    def operands(read, which):
        flats, weighteds = [], []
        for f in range(fold):
            for t in range(each):
                got = read(t).astype(jnp.float32)
                flat = got[:, f * snaps:(f + 1) * snaps].reshape(rows_half, LANES)
                w = weights_ref[pl.ds(slab_start(loc, which) + f * each + t, 1), :]
                flats.append(flat.astype(jnp.bfloat16))
                weighteds.append((flat * w).astype(jnp.bfloat16))
        return flats, weighteds

    flat0, weighted0 = operands(lambda t: snap_own[:, 0, :, t * LANES:(t + 1) * LANES], 0)
    flat1, weighted1 = operands(lambda t: snap_own[:, 1, :, t * LANES:(t + 1) * LANES], 1)
    flat2, weighted2 = operands(lambda t: snap_far[:, :, t * LANES:(t + 1) * LANES], 0)

    def outer(left, right):
        return lax.dot_general(
            jnp.concatenate(left, axis=1), jnp.concatenate(right, axis=1),
            (((1,), (1,)), ((), ())), preferred_element_type=jnp.float32)

    gram_far[...] = outer(weighted2, flat0).reshape(half, snaps, rows_half)

    def give_far(step, carry):
        spot = nth(step)
        far_out[spot] = pack(gram_far[spot]).astype(jnp.bfloat16)
        far_gram(spot, loc).start()
        return carry

    lax.fori_loop(0, half, give_far, 0)
    gram_own[0] = outer(weighted0 + weighted1, flat0 + flat1).reshape(half, snaps, rows_half)
    gram_own[1] = outer(weighted0, flat2).reshape(half, snaps, rows_half)

    def give_own(step, carry):
        spot = nth(step)
        both = jnp.concatenate([gram_own[0, spot], gram_own[1, spot]], axis=1)
        own_out[spot] = pack(both).astype(jnp.bfloat16)
        own_gram(spot, loc).start()
        return carry

    lax.fori_loop(0, half - 1, give_own, 0)
    both = jnp.concatenate([gram_own[0, loc], gram_own[1, loc]], axis=1)
    own_sum = pack(both)

    def take_own(step, total):
        source = nth(step)
        own_gram(loc, source).wait_recv()
        return total + own_in[source].astype(jnp.float32)

    own_sum = lax.fori_loop(0, half - 1, take_own, own_sum)

    def take_far(step, total):
        source = nth(step)
        far_gram(loc, source).wait_recv()
        return total + far_in[source].astype(jnp.float32)

    far_sum = lax.fori_loop(
        0, half, take_far, jnp.zeros(far_in.shape[1:], jnp.float32))
    own = unpack(own_sum, snaps, 2 * rows_half)
    near = own[:, :rows_half]
    far = own[:, rows_half:] + unpack(far_sum, snaps, rows_half)
    out_ref[...] = jnp.where(side == 0, jnp.concatenate([near, far], axis=1),
                             jnp.concatenate([far, near], axis=1))

    def drain(step, carry):
        spot = nth(step)
        own_snap(spot, loc).wait_send()
        own_gram(spot, loc).wait_send()
        far_snap(spot, loc).wait_send()
        far_gram(spot, loc).wait_send()
        return carry

    lax.fori_loop(0, half - 1, drain, 0)
    far_snap(loc, loc).wait_send()
    far_gram(loc, loc).wait_send()


def per_device(n, tile_values, directions, columns, counts, weights):
    _, row_tiles, per_row, size, _ = tile_values.shape
    snaps = directions.shape[1]
    chunk = row_tiles // n
    half = n // 2
    fold = 2 if chunk % 2 == 0 else 1
    slab = (fold * snaps, chunk * size // fold)
    own_rows = packed_rows(snaps, n * snaps)
    far_rows = packed_rows(snaps, half * snaps)
    hbm = pl.BlockSpec(memory_space=pltpu.HBM)
    dma = pltpu.SemaphoreType.DMA
    return pl.pallas_call(
        functools.partial(kernel, n, fold),
        out_shape=jax.ShapeDtypeStruct((snaps, n * snaps), jnp.float32),
        in_specs=[hbm] * 5,
        out_specs=pl.BlockSpec(memory_space=pltpu.VMEM),
        scratch_shapes=[
            pltpu.VMEM(directions.shape, jnp.bfloat16),
            pltpu.SMEM((per_row, row_tiles), jnp.int32),
            pltpu.SMEM((row_tiles,), jnp.int32),
            pltpu.VMEM((row_tiles, size), jnp.float32),
            pltpu.VMEM((row_tiles, per_row, size, size), jnp.bfloat16),
            pltpu.VMEM((row_tiles + 1, snaps, size), jnp.bfloat16),
            pltpu.VMEM((half, 2, *slab), jnp.bfloat16),
            pltpu.VMEM((half, 2, *slab), jnp.bfloat16),
            pltpu.VMEM((half, *slab), jnp.bfloat16),
            pltpu.VMEM((2, half, snaps, half * snaps), jnp.float32),
            pltpu.VMEM((half, snaps, half * snaps), jnp.float32),
            pltpu.VMEM((half, own_rows, LANES), jnp.bfloat16),
            pltpu.VMEM((half, own_rows, LANES), jnp.bfloat16),
            pltpu.VMEM((half, far_rows, LANES), jnp.bfloat16),
            pltpu.VMEM((half, far_rows, LANES), jnp.bfloat16),
            dma((4,)), dma((2, half)),
            *[dma((half,)) for _ in range(8)],
        ],
        compiler_params=pltpu.CompilerParams(
            collective_id=0, has_side_effects=True, vmem_limit_bytes=64 * 2**20),
    )(tile_values, directions, columns.T, counts, weights.reshape(-1, LANES))


def solution(mesh):
    in_specs = (
        P(("groups", "member"), None, None, None, None),
        P(("groups", "member"), None, None),
        P(),
        P(),
        P(),
    )
    out_specs = P(("groups", "member"), None)
    return jax.shard_map(
        functools.partial(per_device, mesh.shape["member"]), mesh=mesh,
        in_specs=in_specs, out_specs=out_specs, check_vma=False
    )
```

time: 98.1 us -> 26.8 us (0.27)
  waiting for transfers between devices: 65.3 us -> 0 us
  Pallas kernels: 0 us -> 25.2 us
  between operations: 13.5 us -> 0.01 us
  starting transfers between devices: 7.43 us -> 0 us
  matrix products: 6.93 us -> 0 us
  local copies, waits for them, and re-layouts: 4.62 us -> 1.39 us
    unnamed x2 -> x0, waiting for transfers between devices: 53.9 us -> none
    pallas_call x0 -> x1, Pallas kernels: none -> 25.2 us  [per_device(): pl.pallas_call(functools.partial(kernel, n, fold), out_shape=jax.ShapeDty...]
    all_to_all x1 -> x0, waiting for transfers between devices: 11.4 us -> none  [per_device(): lax.all_to_all(snaps_local, 'member', split_axis=1, concat_axis=0, tiled=...]
    all_to_all x1 -> x0, starting transfers between devices: 7.39 us -> none  [per_device(): lax.all_to_all(snaps_local, 'member', split_axis=1, concat_axis=0, tiled=...]
    dot_general x2 -> x0, matrix products: 6.93 us -> none  [the longest x1 5.71 us: snapshot(): jnp.einsum('rkij,srkj->sri', tiles_one, picked, preferred_element_type=jn...]
    convert_element_type x3 -> x0, local copies, waits for them, and re-layouts: 1.3 us -> none  [snapshot(): return result.reshape(snaps, row_tiles * tile_size).astype(jnp.bfloat16)]
    gather x1 -> x0, local copies, waits for them, and re-layouts: 0.99 us -> none  [snapshot(): picked = blocks[:, columns, :]]
  transfers between devices with their start and end apart: 2 -> 0, of which waited for: 2 -> 0; matrix products, arithmetic and copies ran while one was open for 1% -> 0% of each run, Pallas kernels for 0% -> 0%
where the time goes in v2:
time: 26.8 us; the launch traced here: 26.6 us
  Pallas kernels  25.2 us (94%)
  local copies, waits for them, and re-layouts  1.39 us (5%)
    pallas_call x1, Pallas kernels, per_device(): pl.pallas_call(functools.partial(kernel, n, fold), out_shape=jax.ShapeDty...  25.2 us
    unnamed x1, local copies, waits for them, and re-layouts  1.39 us

profile of v2, /device:TPU:0, one launch (start us, length us, event | category | flops | bytes accessed | tf_op | source)
XLA Modules:
  0.0 26.6 jit_solution(11469569991013607589)
XLA Ops:
  0.0 25.2 %shard_map.55 = f32[24,384]{1,0:T(8,128)} custom-call(bf16[1,64,4,128,128]{4,3,2,1,0:T(8,128)(2,1)} %tiles_hbm.1, bf16[1,24,8192]{2,1,0:T(8,128)(2,1)} %dirs_hbm.1, s32[4,64]{1,0:T(4,128)} %bitcast.3, s32[64]{0:T(128)} %counts_hbm.1, f32[64,128]{1,0:T(8,128)} %bitcast.2), custom_call_target="tpu_custom_call" | custom-call | tf_op jit(solution)/shard_map/pallas_call | solution.py:255
  25.2 1.4 %copy.7 = f32[24,384]{1,0:T(8,128)} copy(f32[24,384]{1,0:T(8,128)} %shard_map.55) | data formatting | bytes 73728

commit v3 on v2

--- a/solution.py
+++ b/solution.py
@@ -39,9 +39,10 @@
 
 def kernel(n, fold, tiles_hbm, dirs_hbm, cols_hbm, counts_hbm, weights_hbm, out_ref,
            dirs_ref, cols_ref, counts_ref, weights_ref, tiles, dirs,
-           snap_out, snap_own, snap_far, gram_own, gram_far, own_out, own_in, far_out, far_in,
+           snap_out, snap_own, snap_far, gram_near, gram_far, near_out, near_in,
+           cross_out, cross_in, far_out, far_in,
            arg_sem, tile_sem, own_send1, own_recv1, far_send1, far_recv1,
-           own_send2, own_recv2, far_send2, far_recv2):
+           near_send, near_recv, cross_send, cross_recv, far_send2, far_recv2):
     me = lax.axis_index("member")
     per_row, row_tiles = cols_ref.shape
     snaps = dirs_ref.shape[1]
@@ -78,11 +79,15 @@
         return remote(snap_out.at[spot, 1], snap_far.at[source], far_send1.at[spot],
                       far_recv1.at[source], other + spot)
 
-    def own_gram(spot, source):
-        return remote(own_out.at[spot], own_in.at[source], own_send2.at[spot],
-                      own_recv2.at[source], mine + spot)
-
-    def far_gram(spot, source):
+    def near_sum(spot, source):
+        return remote(near_out.at[spot], near_in.at[source], near_send.at[spot],
+                      near_recv.at[source], mine + spot)
+
+    def cross_sum(spot, source):
+        return remote(cross_out.at[spot], cross_in.at[source], cross_send.at[spot],
+                      cross_recv.at[source], mine + spot)
+
+    def far_sum(spot, source):
         return remote(far_out.at[spot], far_in.at[source], far_send2.at[spot],
                       far_recv2.at[source], other + spot)
 
@@ -157,13 +162,11 @@
     tile_copy(half - 1, 0).wait()
     snap_own[loc, 0] = product(loc, 0)
 
-    def land(step, carry):
+    def land_own(step, carry):
         own_snap(loc, nth(step)).wait_recv()
-        far_snap(loc, nth(step)).wait_recv()
-        return carry
-
-    lax.fori_loop(0, half - 1, land, 0)
-    far_snap(loc, loc).wait_recv()
+        return carry
+
+    lax.fori_loop(0, half - 1, land_own, 0)
 
     def operands(read, which):
         flats, weighteds = [], []
@@ -178,67 +181,62 @@
 
     flat0, weighted0 = operands(lambda t: snap_own[:, 0, :, t * LANES:(t + 1) * LANES], 0)
     flat1, weighted1 = operands(lambda t: snap_own[:, 1, :, t * LANES:(t + 1) * LANES], 1)
-    flat2, weighted2 = operands(lambda t: snap_far[:, :, t * LANES:(t + 1) * LANES], 0)
-
     def outer(left, right):
         return lax.dot_general(
             jnp.concatenate(left, axis=1), jnp.concatenate(right, axis=1),
             (((1,), (1,)), ((), ())), preferred_element_type=jnp.float32)
 
-    gram_far[...] = outer(weighted2, flat0).reshape(half, snaps, rows_half)
-
-    def give_far(step, carry):
-        spot = nth(step)
-        far_out[spot] = pack(gram_far[spot]).astype(jnp.bfloat16)
-        far_gram(spot, loc).start()
-        return carry
-
-    lax.fori_loop(0, half, give_far, 0)
-    gram_own[0] = outer(weighted0 + weighted1, flat0 + flat1).reshape(half, snaps, rows_half)
-    gram_own[1] = outer(weighted0, flat2).reshape(half, snaps, rows_half)
-
-    def give_own(step, carry):
-        spot = nth(step)
-        both = jnp.concatenate([gram_own[0, spot], gram_own[1, spot]], axis=1)
-        own_out[spot] = pack(both).astype(jnp.bfloat16)
-        own_gram(spot, loc).start()
-        return carry
-
-    lax.fori_loop(0, half - 1, give_own, 0)
-    both = jnp.concatenate([gram_own[0, loc], gram_own[1, loc]], axis=1)
-    own_sum = pack(both)
-
-    def take_own(step, total):
-        source = nth(step)
-        own_gram(loc, source).wait_recv()
-        return total + own_in[source].astype(jnp.float32)
-
-    own_sum = lax.fori_loop(0, half - 1, take_own, own_sum)
-
-    def take_far(step, total):
-        source = nth(step)
-        far_gram(loc, source).wait_recv()
-        return total + far_in[source].astype(jnp.float32)
-
-    far_sum = lax.fori_loop(
-        0, half, take_far, jnp.zeros(far_in.shape[1:], jnp.float32))
-    own = unpack(own_sum, snaps, 2 * rows_half)
-    near = own[:, :rows_half]
-    far = own[:, rows_half:] + unpack(far_sum, snaps, rows_half)
-    out_ref[...] = jnp.where(side == 0, jnp.concatenate([near, far], axis=1),
-                             jnp.concatenate([far, near], axis=1))
+    def give(gram, out, copy, steps):
+        def send(step, carry):
+            spot = nth(step)
+            out[spot] = pack(gram[spot]).astype(out.dtype)
+            copy(spot, loc).start()
+            return carry
+
+        lax.fori_loop(0, steps, send, 0)
+        return pack(gram[loc])
+
+    def take(arrived, copy, steps, total):
+        def add(step, total):
+            source = nth(step)
+            copy(loc, source).wait_recv()
+            return total + arrived[source].astype(jnp.float32)
+
+        return lax.fori_loop(0, steps, add, total)
+
+    gram_near[...] = outer(weighted0 + weighted1, flat0 + flat1).reshape(gram_near.shape)
+    near = give(gram_near, near_out, near_sum, half - 1)
+
+    def land_far(step, carry):
+        far_snap(loc, nth(step)).wait_recv()
+        return carry
+
+    lax.fori_loop(0, half, land_far, 0)
+    flat2, weighted2 = operands(lambda t: snap_far[:, :, t * LANES:(t + 1) * LANES], 0)
+
+    gram_far[...] = outer(weighted2, flat0).reshape(gram_far.shape)
+    give(gram_far, far_out, far_sum, half)
+    gram_far[...] = outer(weighted0, flat2).reshape(gram_far.shape)
+    cross = give(gram_far, cross_out, cross_sum, half - 1)
+
+    near = unpack(take(near_in, near_sum, half - 1, near), snaps, rows_half)
+    cross = take(cross_in, cross_sum, half - 1, cross)
+    cross = unpack(take(far_in, far_sum, half, cross), snaps, rows_half)
+    out_ref[...] = jnp.where(side == 0, jnp.concatenate([near, cross], axis=1),
+                             jnp.concatenate([cross, near], axis=1))
 
     def drain(step, carry):
         spot = nth(step)
         own_snap(spot, loc).wait_send()
-        own_gram(spot, loc).wait_send()
         far_snap(spot, loc).wait_send()
-        far_gram(spot, loc).wait_send()
+        near_sum(spot, loc).wait_send()
+        cross_sum(spot, loc).wait_send()
+        far_sum(spot, loc).wait_send()
         return carry
 
     lax.fori_loop(0, half - 1, drain, 0)
     far_snap(loc, loc).wait_send()
-    far_gram(loc, loc).wait_send()
+    far_sum(loc, loc).wait_send()
 
 
 def per_device(n, tile_values, directions, columns, counts, weights):
@@ -248,8 +246,7 @@
     half = n // 2
     fold = 2 if chunk % 2 == 0 else 1
     slab = (fold * snaps, chunk * size // fold)
-    own_rows = packed_rows(snaps, n * snaps)
-    far_rows = packed_rows(snaps, half * snaps)
+    block = (packed_rows(snaps, half * snaps), LANES)
     hbm = pl.BlockSpec(memory_space=pltpu.HBM)
     dma = pltpu.SemaphoreType.DMA
     return pl.pallas_call(
@@ -267,14 +264,16 @@
             pltpu.VMEM((half, 2, *slab), jnp.bfloat16),
             pltpu.VMEM((half, 2, *slab), jnp.bfloat16),
             pltpu.VMEM((half, *slab), jnp.bfloat16),
-            pltpu.VMEM((2, half, snaps, half * snaps), jnp.float32),
             pltpu.VMEM((half, snaps, half * snaps), jnp.float32),
-            pltpu.VMEM((half, own_rows, LANES), jnp.bfloat16),
-            pltpu.VMEM((half, own_rows, LANES), jnp.bfloat16),
-            pltpu.VMEM((half, far_rows, LANES), jnp.bfloat16),
-            pltpu.VMEM((half, far_rows, LANES), jnp.bfloat16),
+            pltpu.VMEM((half, snaps, half * snaps), jnp.float32),
+            pltpu.VMEM((half, *block), jnp.bfloat16),
+            pltpu.VMEM((half, *block), jnp.bfloat16),
+            pltpu.VMEM((half, *block), jnp.bfloat16),
+            pltpu.VMEM((half, *block), jnp.bfloat16),
+            pltpu.VMEM((half, *block), jnp.bfloat16),
+            pltpu.VMEM((half, *block), jnp.bfloat16),
             dma((4,)), dma((2, half)),
-            *[dma((half,)) for _ in range(8)],
+            *[dma((half,)) for _ in range(10)],
         ],
         compiler_params=pltpu.CompilerParams(
             collective_id=0, has_side_effects=True, vmem_limit_bytes=64 * 2**20),

time: 26.8 us -> 26.3 us (0.981)
  Pallas kernels: 25.2 us -> 24.7 us
    pallas_call x1, Pallas kernels: 25.2 us -> 24.7 us  [per_device(): pl.pallas_call(functools.partial(kernel, n, fold), out_shape=jax.ShapeDty...]
where the time goes in v3:
time: 26.3 us; the launch traced here: 26.1 us
  Pallas kernels  24.7 us (94%)
  local copies, waits for them, and re-layouts  1.39 us (5%)
    pallas_call x1, Pallas kernels, per_device(): pl.pallas_call(functools.partial(kernel, n, fold), out_shape=jax.ShapeDty...  24.7 us
    unnamed x1, local copies, waits for them, and re-layouts  1.39 us

profile of v3, /device:TPU:0, one launch (start us, length us, event | category | flops | bytes accessed | tf_op | source)
XLA Modules:
  0.0 26.1 jit_solution(2111163483062610306)
XLA Ops:
  0.0 24.7 %shard_map.55 = f32[24,384]{1,0:T(8,128)} custom-call(bf16[1,64,4,128,128]{4,3,2,1,0:T(8,128)(2,1)} %tiles_hbm.1, bf16[1,24,8192]{2,1,0:T(8,128)(2,1)} %dirs_hbm.1, s32[4,64]{1,0:T(4,128)} %bitcast.3, s32[64]{0:T(128)} %counts_hbm.1, f32[64,128]{1,0:T(8,128)} %bitcast.2), custom_call_target="tpu_custom_call" | custom-call | tf_op jit(solution)/shard_map/pallas_call | solution.py:252
  24.7 1.4 %copy.7 = f32[24,384]{1,0:T(8,128)} copy(f32[24,384]{1,0:T(8,128)} %shard_map.55) | data formatting | bytes 73728
